TPU v7x, 32 devices: a whole 2x2x4 slice. The times are simulated.
32 devices in a mesh: outer: 2 (over x), sec: 8 (over z, core), tp: 2 (over y).
Axes of the slice: x: 2, y: 2, z: 4, core: 2. Of those that a mesh axis runs over, the one named last changes fastest.
Arguments:
- tile_maps: bfloat16 [32, 12, 12, 3072], P(('outer', 'sec'), None, None, 'tp'), may hold values from -6 to 6
- tile_shape: int32 [32, 2], P(('outer', 'sec')), may hold values from 4 to 12
- conv_kernel: float32 [7, 7, 3072], P(None, None, 'tp'), may hold values from -0.875 to 0.875
- norm_gain: float32 [3072], P('tp'), may hold values from 0.25 to 1.75
- norm_bias: float32 [3072], P('tp'), may hold values from -3 to 3
- projector: bfloat16 [3072, 7168], P('tp', 'sec'), may hold values from -0.109375 to 0.109375
- text_rows: bfloat16 [9216, 7168], P(('outer', 'sec'), 'tp'), may hold values from -6 to 6
- row_order: int32 [16, 576], P(('outer', 'sec')), may hold values from 0 to 575, each once within a row
- seq_gain: float32 [7168], P('tp'), may hold values from 0.25 to 1.75
- cotangent: bfloat16 [9216, 7168], P(('outer', 'sec'), 'tp'), may hold values from -0.2772166 to 0.2772166, as said below
Outputs:
- normed: bfloat16 [9216, 7168], P(('outer', 'sec'), 'tp')
- kernel_delta: float32 [7, 7, 3072], P(None, None, 'tp')
- gain_delta: float32 [3072], P('tp')
- bias_delta: float32 [3072], P('tp')
Inputs may be any that keep to these rules, and one draw needn't show every extreme that they name: `row_order`: each row lists where the visual tokens arriving at that device stand, in arrival order, then the text rows. `tile_shape`: valid rows and columns of each tile, the rest of the map is padding. `cotangent`: gradient of the training loss.
All inputs are finite; a program needn't handle non-finite values.
Results may differ from a plain program's by a relative error of at most 0.0043.
Values may be sent and summed in bfloat16 or wider, within the bound.
A program may use at most 128 MiB of HBM per device.

v0:
```python
import jax
import jax.numpy as jnp
from jax import lax
from jax.sharding import PartitionSpec as P


def shape_mask(tile_shape, grid):
    places = lax.broadcasted_iota(jnp.int32, (1, grid), 1)
    rows_ok = places < tile_shape[:, 0:1]
    cols_ok = places < tile_shape[:, 1:2]
    return (rows_ok[:, :, None] & cols_ok[:, None, :]).astype(jnp.float32)


def on_device(
    tile_maps,
    tile_shape,
    conv_kernel,
    norm_gain,
    norm_bias,
    projector,
    text_rows,
    row_order,
    seq_gain,
    cotangent,
):
    grid = tile_maps.shape[1]
    half_ch = tile_maps.shape[3]
    channels = half_ch * lax.axis_size("tp")
    rows_dev = tile_maps.shape[0] * grid * grid
    width = text_rows.shape[1] * lax.axis_size("tp")
    validity = shape_mask(tile_shape, grid)[..., None]
    masked = tile_maps.astype(jnp.float32) * validity
    padded = jnp.pad(masked, ((0, 0), (3, 3), (3, 3), (0, 0)))
    conv_out = jnp.zeros(masked.shape, jnp.float32)
    for row_off in range(7):
        for col_off in range(7):
            conv_out = (
                conv_out
                + padded[:, row_off : row_off + grid, col_off : col_off + grid, :]
                * conv_kernel[row_off, col_off]
            )
    total_one, total_two = lax.psum(
        (jnp.sum(conv_out, axis=-1), jnp.sum(conv_out * conv_out, axis=-1)), "tp"
    )
    center = (total_one / channels)[..., None]
    inverse = lax.rsqrt((total_two / channels)[..., None] - center * center + 1e-06)
    normal = (conv_out - center) * inverse
    features = (
        (validity * (normal * norm_gain + norm_bias))
        .astype(jnp.bfloat16)
        .reshape(rows_dev, half_ch)
    )
    whole_weight = lax.all_gather(projector, "sec", axis=1, tiled=True)
    partial_value = jnp.dot(features, whole_weight, preferred_element_type=jnp.float32)
    visual = lax.psum_scatter(partial_value, "tp", scatter_dimension=1, tiled=True).astype(
        jnp.bfloat16
    )
    arrived = lax.all_to_all(visual, "sec", split_axis=0, concat_axis=0, tiled=True)
    positions = row_order[0, :rows_dev]
    merged = text_rows.at[positions].set(arrived)
    wide = merged.astype(jnp.float32)
    upstream = cotangent.astype(jnp.float32) * seq_gain
    square_sum, along = lax.psum(
        (jnp.sum(wide * wide, axis=-1), jnp.sum(upstream * wide, axis=-1)), "tp"
    )
    inv_rms = lax.rsqrt(square_sum / width + 1e-05)[:, None]
    normed = (wide * inv_rms * seq_gain).astype(jnp.bfloat16)
    grad_seq = inv_rms * upstream - wide * (inv_rms * inv_rms * inv_rms) * along[:, None] / width
    picked = grad_seq[positions].astype(jnp.bfloat16)
    returned = lax.all_to_all(picked, "sec", split_axis=0, concat_axis=0, tiled=True)
    full_grad = lax.all_gather(returned, "tp", axis=1, tiled=True)
    grad_rows = jnp.dot(full_grad, whole_weight.T, preferred_element_type=jnp.float32)
    masked_grad = grad_rows.reshape(masked.shape) * validity
    scaled = masked_grad * norm_gain
    first_sum, second_sum = lax.psum(
        (jnp.sum(scaled, axis=-1), jnp.sum(scaled * normal, axis=-1)), "tp"
    )
    grad_conv = inverse * (
        scaled - (first_sum / channels)[..., None] - normal * (second_sum / channels)[..., None]
    )
    kernel_rows = []
    for row_off in range(7):
        for col_off in range(7):
            window = padded[:, row_off : row_off + grid, col_off : col_off + grid, :]
            kernel_rows.append(jnp.sum(window * grad_conv, axis=(0, 1, 2)))
    gain_grad = jnp.sum(masked_grad * normal, axis=(0, 1, 2))
    bias_grad = jnp.sum(masked_grad, axis=(0, 1, 2))
    local_delta = jnp.stack(kernel_rows + [gain_grad, bias_grad], axis=0)
    pods = lax.axis_size("outer")
    entries = 51 * channels
    pod_sum = lax.psum(local_delta, "sec")
    norm_sq = lax.psum(jnp.sum(pod_sum * pod_sum), "tp")
    factor = jnp.minimum(1.0, 1.0 / jnp.sqrt(norm_sq / entries + 1e-06))
    average = lax.psum(pod_sum * factor, "outer") / pods
    return (normed, average[:49].reshape(7, 7, half_ch), average[49], average[50])


def solution(mesh):
    in_specs = (
        P(("outer", "sec"), None, None, "tp"),
        P(("outer", "sec"), None),
        P(None, None, "tp"),
        P("tp"),
        P("tp"),
        P("tp", "sec"),
        P(("outer", "sec"), "tp"),
        P(("outer", "sec"), None),
        P("tp"),
        P(("outer", "sec"), "tp"),
    )
    out_specs = (P(("outer", "sec"), "tp"), P(None, None, "tp"), P("tp"), P("tp"))
    return jax.shard_map(
        on_device, mesh=mesh, in_specs=in_specs, out_specs=out_specs, check_vma=False
    )
```

profile of v0, /device:TPU:0, one launch (start us, length us, event | category | flops | bytes accessed | tf_op | source)
XLA Modules:
  0.0 696.8 jit_solution(15552070662868830435)
XLA Ops:
  7.2 0.0 all-gather.3.cloned.1.call-start
  7.2 4.4 copy.23
  11.6 0.0 all-gather.3.cloned.1.call-update
  11.7 0.0 reduce-scatter.2.cloned.1.call-start
  11.7 0.6 copy-done.9
  12.3 0.2 slice_reduce_fusion.52
  12.5 0.1 copy-done.2
  12.6 0.2 slice_reduce_fusion.48
  12.8 0.3 slice_reduce_fusion.50
  13.1 0.9 slice_reduce_fusion.49
  14.0 0.1 iota_compare_fusion
  14.1 0.1 and_convert_fusion
  14.2 0.2 convert_multiply_fusion.5
  14.4 23.6 %fusion.8 = (f32[2,12,12]{2,1,0:T(8,128)S(1)}, f32[2,12,12]{2,1,0:T(8,128)S(1)}, f32[2,12,12,1536]{3,2,1,0:T(8,128)}) fusion(f32[1536]{0:T(1024)S(1)} %get-tuple-element.110, f32[1536]{0:T(1024)S(1)} %get-tuple-element.111, f32[1536]{0:T(1024)S(1)} %get-tuple-element.64, f32[1536]{0:T(1024)S(1)} %get-tuple-element.65, f32[1536]{0:T(1024)S(1)} %get-tuple-element.66, ...), kind=kLoop, calls=%fused_computation.189 | loop fusion | flops 44236224 | bytes 3842304 | tf_op jit(solution)/shard_map/reduce_sum | solution.py:43
  38.1 9.8 %all-reduce.3 = (f32[2,12,12]{2,1,0:T(8,128)S(1)}, f32[2,12,12]{2,1,0:T(8,128)S(1)}) all-reduce(f32[2,12,12]{2,1,0:T(8,128)S(1)} %get-tuple-element.58, f32[2,12,12]{2,1,0:T(8,128)S(1)} %get-tuple-element.57), channel_id=1, replica_groups=mesh['outer'=2,'sec'=8,'tp'=2] {'tp'}, use_global_device_ids=true, to_apply=%region_3.4 | all-reduce | flops 576 | bytes 4608 | tf_op jit(solution)/shard_map/psum | solution.py:42
  47.9 0.0 copy-start.5
  47.9 0.6 copy-done.3
  48.5 0.0 copy-done.5
  48.5 3.5 multiply_convert_fusion
  52.0 1.1 reshape.168
  53.1 155.4 %all-gather.3.cloned.1.call-done = bf16[1536,7168]{1,0:T(8,128)(2,1)} async-done(((bf16[1536,896]{1,0:T(8,128)(2,1)}), bf16[1536,7168]{1,0:T(8,128)(2,1)}) %all-gather.3.cloned.1.call-update) | async-done | bytes 22020112 | tf_op jit(solution)/shard_map/all_gather | solution.py:53
  208.5 13.1 %fusion.9 = f32[288,7168]{1,0:T(8,128)} fusion(bf16[288,1536]{1,0:T(8,128)(2,1)} %reshape.168, bf16[1536,7168]{1,0:T(8,128)(2,1)} %all-gather.3.cloned.1.call-done), kind=kOutput, calls=%fused_computation.190 | convolution fusion | flops 6341787648 | bytes 31162368 | tf_op jit(solution)/shard_map/dot_general | solution.py:54
  221.7 0.0 reduce-scatter.2.cloned.1.call-update
  221.7 96.2 %reduce-scatter.2.cloned.1.call-done = f32[288,3584]{1,0:T(8,128)} async-done(((f32[288,7168]{1,0:T(8,128)}), f32[288,3584]{1,0:T(8,128)}) %reduce-scatter.2.cloned.1.call-update) | async-done | bytes 4128784 | tf_op jit(solution)/shard_map/reduce_scatter | solution.py:55
  317.8 3.7 convert_element_type.43
  321.6 4.0 all_to_all.14
  325.5 4.7 all-to-all-start
  330.3 0.2 all-gather.5.cloned.1.call-start
  330.5 53.1 %all-to-all-done = bf16[8,36,3584]{2,1,0:T(8,128)(2,1)} async-done(((bf16[8,36,3584]{2,1,0:T(8,128)(2,1)}), bf16[8,36,3584]{2,1,0:T(8,128)(2,1)}, u32[]{:S(2)}, u32[]{:S(2)}) %all-to-all-start) | async-done | bytes 2064416 | tf_op jit(solution)/shard_map/all_to_all | solution.py:58
  383.7 4.0 reshape.184
  387.7 9.2 %scatter_fusion = bf16[576,3584]{1,0:T(8,128)(2,1)} fusion(bf16[576,3584]{1,0:T(8,128)(2,1)} %copy.23, s32[288]{0:T(512)S(1)} %fusion.7, bf16[288,3584]{1,0:T(8,128)(2,1)} %reshape.184), kind=kCustom, calls=%fused_computation.1 | custom fusion | bytes 6194304 | tf_op jit(solution)/shard_map/scatter | solution.py:60
  396.9 5.4 fusion.6
  402.3 5.0 all-reduce.2
  407.3 6.7 fusion.5
  414.0 10.0 %gather_fusion = bf16[288,3584]{1,0:T(8,128)(2,1)} fusion(bf16[576,3584]{1,0:T(8,128)(2,1)} %fusion.5, s32[1024]{0:T(1024)S(1)} %pad_clamp_fusion), kind=kCustom, calls=%fused_computation | custom fusion | bytes 4129920 | tf_op jit(solution)/shard_map/gather | solution.py:69
  424.1 4.0 convert_element_type.48
  428.0 57.6 %all_to_all.21 = bf16[8,36,3584]{2,1,0:T(8,128)(2,1)} all-to-all(bf16[8,36,3584]{2,1,0:T(8,128)(2,1)} %convert_element_type.48), channel_id=1, replica_groups=mesh['outer'=2,'sec'=8,'tp'=2] {'sec'}, dimensions={0} | all-to-all | bytes 4128768 | tf_op jit(solution)/shard_map/all_to_all | solution.py:70
  485.7 4.0 all_to_all.18
  489.6 0.0 all-gather.5.cloned.1.call-update
  489.6 0.0 all-reduce.7.cloned.1.call-start
  489.7 0.1 reshape.171
  489.8 54.0 %all-gather.5.cloned.1.call-done = bf16[288,7168]{1,0:T(8,128)(2,1)} async-done(((bf16[288,3584]{1,0:T(8,128)(2,1)}), bf16[288,7168]{1,0:T(8,128)(2,1)}) %all-gather.5.cloned.1.call-update) | async-done | bytes 4128784 | tf_op jit(solution)/shard_map/all_gather | solution.py:71
  543.7 13.2 %multiply_reduce_fusion.53 = (f32[1536]{0:T(1024)S(1)}, f32[288]{0:T(512)S(1)}, f32[288,1536]{1,0:T(8,128)}) fusion(f32[288]{0:T(512)S(1)} %reshape.171, f32[1536]{0:T(1024)S(1)} %copy-done.8, bf16[288,7168]{1,0:T(8,128)(2,1)} %all-gather.5.cloned.1.call-done, bf16[1536,7168]{1,0:T(8,128)(2,1)} %all-gather.3.cloned.1.call-done), kind=kOutput, calls=%fused_computation.120 | convolution fusion | flops 6343555072 | bytes 27932928 | tf_op jit(solution)/shard_map/dot_general | solution.py:72
  557.0 2.8 reshape.169
  559.8 3.4 multiply_reduce_fusion
  563.1 0.1 reduce_sum.529
  563.2 7.4 %all-reduce.1 = (f32[2,12,12]{2,1,0:T(8,128)S(1)}, f32[2,12,12]{2,1,0:T(8,128)S(1)}) all-reduce(f32[2,12,12]{2,1,0:T(8,128)S(1)} %get-tuple-element.5, f32[2,12,12]{2,1,0:T(8,128)S(1)} %reduce_sum.529), channel_id=1, replica_groups=mesh['outer'=2,'sec'=8,'tp'=2] {'tp'}, use_global_device_ids=true, to_apply=%region_13.14 | all-reduce | flops 576 | bytes 4608 | tf_op jit(solution)/shard_map/psum | solution.py:75
  570.7 9.6 %multiply_reduce_fusion.1 = (f32[1536]{0:T(1024)S(1)}, f32[1536]{0:T(1024)S(1)}, f32[1536]{0:T(1024)S(1)}, f32[1536]{0:T(1024)S(1)}, f32[1536]{0:T(1024)S(1)}, /...) fusion(f32[2,12,12,1536]{3,2,1,0:T(8,128)S(1)} %convert_multipl, ...), kind=kLoop, calls=%fused_computation.63 | loop fusion | flops 19436544 | bytes 7200384 | tf_op jit(solution)/shard_map/reduce_sum | solution.py:85
  580.3 0.0 copy-start.1
  580.3 6.3 multiply_reduce_fusion.19
  586.6 5.4 multiply_reduce_fusion.38
  592.8 4.8 stack.207
  597.6 0.0 all-reduce.7.cloned.1.call-update
  597.6 0.0 all-reduce.9.cloned.1.call-start
  597.7 54.4 %all-reduce.7.cloned.1.call-done = f32[51,1536]{1,0:T(8,128)} async-done(((f32[51,1536]{1,0:T(8,128)}), f32[51,1536]{1,0:T(8,128)}) %all-reduce.7.cloned.1.call-update) | async-done | bytes 313360 | tf_op jit(solution)/shard_map/psum | solution.py:91
  652.0 1.7 multiply_reduce_fusion.54
  653.7 5.5 psum.70
  660.0 1.7 broadcast_multiply_fusion.1
  661.7 0.0 all-reduce.9.cloned.1.call-update
  661.7 5.5 fusion.2
  667.2 20.6 %all-reduce.9.cloned.1.call-done = f32[51,1536]{1,0:T(8,128)} async-done(((f32[51,1536]{1,0:T(8,128)}), f32[51,1536]{1,0:T(8,128)}) %all-reduce.9.cloned.1.call-update) | async-done | bytes 313360 | tf_op jit(solution)/shard_map/psum | solution.py:94
  687.9 1.0 broadcast_multiply_fusion
  688.9 0.6 slice_reduce_fusion
  689.5 0.8 reshape.170
  (73 shorter events, 0.4 us)
Async XLA Ops:
  7.2 201.4 %all-gather.3.cloned.1.call-start = ((), (), s32[]{:S(2)}) async-start(), calls=%async_computation.3 | async-start | bytes 24772608 | tf_op jit(solution)/shard_map/all_gather | solution.py:53
  11.6 0.7 copy-start.9
  11.6 1.0 copy-start.2
  11.6 2.6 copy-start
  11.7 306.2 %reduce-scatter.2.cloned.1.call-start = ((), (), s32[]{:S(2)}) async-start(), calls=%async_computation.4 | async-start | bytes 12386304 | tf_op jit(solution)/shard_map/reduce_scatter | solution.py:55
  47.9 0.6 copy-start.3
  47.9 0.6 copy-start.5
  325.5 5.0 copy-start.10
  325.5 58.1 %all-to-all-start = ((bf16[8,36,3584]{2,1,0:T(8,128)(2,1)}), bf16[8,36,3584]{2,1,0:T(8,128)(2,1)}, u32[]{:S(2)}, u32[]{:S(2)}) async-start(bf16[8,36,3584]{2,1,0:T(8,128)(2,1)} %all_to_all.14), calls=%async_computation.1 | async-start | bytes 4587520 | tf_op jit(solution)/shard_map/all_to_all | solution.py:58
  330.3 213.5 %all-gather.5.cloned.1.call-start = ((), (), s32[]{:S(2)}) async-start(), calls=%async_computation.5 | async-start | bytes 6193152 | tf_op jit(solution)/shard_map/all_gather | solution.py:71
  387.7 9.2 %copy-start.7 = (f32[3584]{0:T(1024)S(1)}, f32[3584]{0:T(1024)}, u32[]{:S(2)}) copy-start(f32[3584]{0:T(1024)} %param.18) | copy-start | bytes 43012
  485.6 58.1 %copy-start.8 = (f32[1536]{0:T(1024)S(1)}, f32[1536]{0:T(1024)}, u32[]{:S(2)}) copy-start(f32[1536]{0:T(1024)} %param.13) | copy-start | bytes 18436
  489.6 162.4 %all-reduce.7.cloned.1.call-start = ((), (), s32[]{:S(2)}) async-start(), calls=%async_computation.6 | async-start | bytes 688128 | tf_op jit(solution)/shard_map/psum | solution.py:91
  557.0 2.8 copy-start.4
  557.0 2.8 copy-start.6
  580.3 6.4 copy-start.1
  597.6 90.2 %all-reduce.9.cloned.1.call-start = ((), (), s32[]{:S(2)}) async-start(), calls=%async_computation.7 | async-start | bytes 688128 | tf_op jit(solution)/shard_map/psum | solution.py:94
Sparse Core Ops, SparseCore 0:
  11.8 196.7 all-gather.2
  221.8 96.0 reduce-scatter.1
  489.8 53.9 all-gather.4
  597.7 54.2 all-reduce.6
  661.8 25.9 all-reduce.8
where the time goes:
time: 698 us; the launch traced here: 697 us
  waiting for transfers between devices  434 us (62%)
  blocking collectives  85.4 us (12%)
  other arithmetic  78 us (11%)
  local copies, waits for them, and re-layouts  53.2 us (8%)
  matrix products  26.4 us (4%)
  between operations  15 us (2%)
    all_gather x1, waiting for transfers between devices, on_device(): whole_weight = lax.all_gather(projector, 'sec', axis=1, tiled=True)  155 us
    reduce_scatter x1, waiting for transfers between devices, on_device(): lax.psum_scatter(partial_value, 'tp', scatter_dimension=1, tiled=True)  96.2 us
    all_to_all x1, blocking collectives, on_device(): lax.all_to_all(picked, 'sec', split_axis=0, concat_axis=0, tiled=True)  57.6 us
    psum x1, waiting for transfers between devices, on_device(): pod_sum = lax.psum(local_delta, 'sec')  54.4 us
    all_gather x1, waiting for transfers between devices, on_device(): full_grad = lax.all_gather(returned, 'tp', axis=1, tiled=True)  54 us
    all_to_all x1, waiting for transfers between devices, on_device(): lax.all_to_all(visual, 'sec', split_axis=0, concat_axis=0, tiled=True)  53.1 us
    reduce_sum x1, other arithmetic, on_device(): jnp.sum(conv_out, axis=-1)  23.6 us
    reduce_sum x3, other arithmetic, on_device(): kernel_rows.append(jnp.sum(window * grad_conv, axis=(0, 1, 2)))  21.3 us
  transfers between devices with their start and end apart: 6, of which 6 were waited for; matrix products, arithmetic and copies ran while one was open for 5% of the time, Pallas kernels for 0%

commit v1 on v0

--- a/solution.py
+++ b/solution.py
@@ -88,7 +88,7 @@
     local_delta = jnp.stack(kernel_rows + [gain_grad, bias_grad], axis=0)
     pods = lax.axis_size("outer")
     entries = 51 * channels
-    pod_sum = lax.psum(local_delta, "sec")
+    pod_sum = jnp.sum(lax.all_gather(local_delta, "sec"), axis=0)
     norm_sq = lax.psum(jnp.sum(pod_sum * pod_sum), "tp")
     factor = jnp.minimum(1.0, 1.0 / jnp.sqrt(norm_sq / entries + 1e-06))
     average = lax.psum(pod_sum * factor, "outer") / pods

time: 698 us -> 677 us (0.970)
  waiting for transfers between devices: 434 us -> 413 us
    psum x1 -> x0, waiting for transfers between devices: 54.4 us -> none  [on_device(): pod_sum = lax.psum(local_delta, 'sec')]
    all_gather x0 -> x1, waiting for transfers between devices: none -> 36.3 us  [on_device(): pod_sum = jnp.sum(lax.all_gather(local_delta, 'sec'), axis=0)]
where the time goes in v1:
time: 677 us; the launch traced here: 676 us
  waiting for transfers between devices  413 us (61%)
  blocking collectives  85.4 us (13%)
  other arithmetic  78 us (12%)
  local copies, waits for them, and re-layouts  53.2 us (8%)
  matrix products  26.4 us (4%)
  between operations  15 us (2%)
    all_gather x1, waiting for transfers between devices, on_device(): whole_weight = lax.all_gather(projector, 'sec', axis=1, tiled=True)  155 us
    reduce_scatter x1, waiting for transfers between devices, on_device(): lax.psum_scatter(partial_value, 'tp', scatter_dimension=1, tiled=True)  96.2 us
    all_to_all x1, blocking collectives, on_device(): lax.all_to_all(picked, 'sec', split_axis=0, concat_axis=0, tiled=True)  57.6 us
    all_gather x1, waiting for transfers between devices, on_device(): full_grad = lax.all_gather(returned, 'tp', axis=1, tiled=True)  54 us
    all_to_all x1, waiting for transfers between devices, on_device(): lax.all_to_all(visual, 'sec', split_axis=0, concat_axis=0, tiled=True)  53.1 us
    all_gather x1, waiting for transfers between devices, on_device(): pod_sum = jnp.sum(lax.all_gather(local_delta, 'sec'), axis=0)  36.3 us
    reduce_sum x1, other arithmetic, on_device(): jnp.sum(conv_out, axis=-1)  23.6 us
    reduce_sum x3, other arithmetic, on_device(): kernel_rows.append(jnp.sum(window * grad_conv, axis=(0, 1, 2)))  21.3 us
  transfers between devices with their start and end apart: 6, of which 6 were waited for; matrix products, arithmetic and copies ran while one was open for 5% of the time, Pallas kernels for 0%

profile of v1, /device:TPU:0, one launch (start us, length us, event | category | flops | bytes accessed | tf_op | source)
XLA Modules:
  0.0 676.3 jit_solution(6664848680185500515)
XLA Ops:
  7.2 0.0 all-gather.6.cloned.1.call-start
  7.2 4.4 copy.23
  11.6 0.0 all-gather.6.cloned.1.call-update
  11.7 0.0 reduce-scatter.2.cloned.1.call-start
  11.7 0.6 copy-done.9
  12.3 0.2 slice_reduce_fusion.52
  12.5 0.1 copy-done.2
  12.6 0.2 slice_reduce_fusion.48
  12.8 0.3 slice_reduce_fusion.50
  13.1 0.9 slice_reduce_fusion.49
  14.0 0.1 iota_compare_fusion
  14.1 0.1 and_convert_fusion
  14.2 0.2 convert_multiply_fusion.5
  14.4 23.6 %fusion.8 = (f32[2,12,12]{2,1,0:T(8,128)S(1)}, f32[2,12,12]{2,1,0:T(8,128)S(1)}, f32[2,12,12,1536]{3,2,1,0:T(8,128)}) fusion(f32[1536]{0:T(1024)S(1)} %get-tuple-element.110, f32[1536]{0:T(1024)S(1)} %get-tuple-element.111, f32[1536]{0:T(1024)S(1)} %get-tuple-element.64, f32[1536]{0:T(1024)S(1)} %get-tuple-element.65, f32[1536]{0:T(1024)S(1)} %get-tuple-element.66, ...), kind=kLoop, calls=%fused_computation.189 | loop fusion | flops 44236224 | bytes 3842304 | tf_op jit(solution)/shard_map/reduce_sum | solution.py:43
  38.1 9.8 %all-reduce.3 = (f32[2,12,12]{2,1,0:T(8,128)S(1)}, f32[2,12,12]{2,1,0:T(8,128)S(1)}) all-reduce(f32[2,12,12]{2,1,0:T(8,128)S(1)} %get-tuple-element.58, f32[2,12,12]{2,1,0:T(8,128)S(1)} %get-tuple-element.57), channel_id=1, replica_groups=mesh['outer'=2,'sec'=8,'tp'=2] {'tp'}, use_global_device_ids=true, to_apply=%region_3.4 | all-reduce | flops 576 | bytes 4608 | tf_op jit(solution)/shard_map/psum | solution.py:42
  47.9 0.0 copy-start.5
  47.9 0.6 copy-done.3
  48.5 0.0 copy-done.5
  48.5 3.5 multiply_convert_fusion
  52.0 1.1 reshape.168
  53.1 155.4 %all-gather.6.cloned.1.call-done = bf16[1536,7168]{1,0:T(8,128)(2,1)} async-done(((bf16[1536,896]{1,0:T(8,128)(2,1)}), bf16[1536,7168]{1,0:T(8,128)(2,1)}) %all-gather.6.cloned.1.call-update) | async-done | bytes 22020112 | tf_op jit(solution)/shard_map/all_gather | solution.py:53
  208.5 13.1 %fusion.9 = f32[288,7168]{1,0:T(8,128)} fusion(bf16[288,1536]{1,0:T(8,128)(2,1)} %reshape.168, bf16[1536,7168]{1,0:T(8,128)(2,1)} %all-gather.6.cloned.1.call-done), kind=kOutput, calls=%fused_computation.190 | convolution fusion | flops 6341787648 | bytes 31162368 | tf_op jit(solution)/shard_map/dot_general | solution.py:54
  221.7 0.0 reduce-scatter.2.cloned.1.call-update
  221.7 96.2 %reduce-scatter.2.cloned.1.call-done = f32[288,3584]{1,0:T(8,128)} async-done(((f32[288,7168]{1,0:T(8,128)}), f32[288,3584]{1,0:T(8,128)}) %reduce-scatter.2.cloned.1.call-update) | async-done | bytes 4128784 | tf_op jit(solution)/shard_map/reduce_scatter | solution.py:55
  317.8 3.7 convert_element_type.43
  321.6 4.0 all_to_all.14
  325.5 4.7 all-to-all-start
  330.3 0.2 all-gather.8.cloned.1.call-start
  330.5 53.1 %all-to-all-done = bf16[8,36,3584]{2,1,0:T(8,128)(2,1)} async-done(((bf16[8,36,3584]{2,1,0:T(8,128)(2,1)}), bf16[8,36,3584]{2,1,0:T(8,128)(2,1)}, u32[]{:S(2)}, u32[]{:S(2)}) %all-to-all-start) | async-done | bytes 2064416 | tf_op jit(solution)/shard_map/all_to_all | solution.py:58
  383.7 4.0 reshape.184
  387.7 9.2 %scatter_fusion = bf16[576,3584]{1,0:T(8,128)(2,1)} fusion(bf16[576,3584]{1,0:T(8,128)(2,1)} %copy.23, s32[288]{0:T(512)S(1)} %fusion.7, bf16[288,3584]{1,0:T(8,128)(2,1)} %reshape.184), kind=kCustom, calls=%fused_computation.1 | custom fusion | bytes 6194304 | tf_op jit(solution)/shard_map/scatter | solution.py:60
  396.9 5.4 fusion.6
  402.3 5.0 all-reduce.2
  407.3 6.7 fusion.5
  414.0 10.0 %gather_fusion = bf16[288,3584]{1,0:T(8,128)(2,1)} fusion(bf16[576,3584]{1,0:T(8,128)(2,1)} %fusion.5, s32[1024]{0:T(1024)S(1)} %pad_clamp_fusion), kind=kCustom, calls=%fused_computation | custom fusion | bytes 4129920 | tf_op jit(solution)/shard_map/gather | solution.py:69
  424.1 4.0 convert_element_type.48
  428.0 57.6 %all_to_all.21 = bf16[8,36,3584]{2,1,0:T(8,128)(2,1)} all-to-all(bf16[8,36,3584]{2,1,0:T(8,128)(2,1)} %convert_element_type.48), channel_id=1, replica_groups=mesh['outer'=2,'sec'=8,'tp'=2] {'sec'}, dimensions={0} | all-to-all | bytes 4128768 | tf_op jit(solution)/shard_map/all_to_all | solution.py:70
  485.7 4.0 all_to_all.18
  489.6 0.0 all-gather.8.cloned.1.call-update
  489.6 0.0 all-gather.10.cloned.1.call-start
  489.7 0.1 reshape.171
  489.8 54.0 %all-gather.8.cloned.1.call-done = bf16[288,7168]{1,0:T(8,128)(2,1)} async-done(((bf16[288,3584]{1,0:T(8,128)(2,1)}), bf16[288,7168]{1,0:T(8,128)(2,1)}) %all-gather.8.cloned.1.call-update) | async-done | bytes 4128784 | tf_op jit(solution)/shard_map/all_gather | solution.py:71
  543.7 13.2 %multiply_reduce_fusion.53 = (f32[1536]{0:T(1024)S(1)}, f32[288]{0:T(512)S(1)}, f32[288,1536]{1,0:T(8,128)}) fusion(f32[288]{0:T(512)S(1)} %reshape.171, f32[1536]{0:T(1024)S(1)} %copy-done.8, bf16[288,7168]{1,0:T(8,128)(2,1)} %all-gather.8.cloned.1.call-done, bf16[1536,7168]{1,0:T(8,128)(2,1)} %all-gather.6.cloned.1.call-done), kind=kOutput, calls=%fused_computation.120 | convolution fusion | flops 6343555072 | bytes 27932928 | tf_op jit(solution)/shard_map/dot_general | solution.py:72
  557.0 2.8 reshape.169
  559.8 3.4 multiply_reduce_fusion
  563.1 0.1 reduce_sum.538
  563.2 7.4 %all-reduce.1 = (f32[2,12,12]{2,1,0:T(8,128)S(1)}, f32[2,12,12]{2,1,0:T(8,128)S(1)}) all-reduce(f32[2,12,12]{2,1,0:T(8,128)S(1)} %get-tuple-element.5, f32[2,12,12]{2,1,0:T(8,128)S(1)} %reduce_sum.538), channel_id=1, replica_groups=mesh['outer'=2,'sec'=8,'tp'=2] {'tp'}, use_global_device_ids=true, to_apply=%region_13.14 | all-reduce | flops 576 | bytes 4608 | tf_op jit(solution)/shard_map/psum | solution.py:75
  570.7 9.6 %multiply_reduce_fusion.1 = (f32[1536]{0:T(1024)S(1)}, f32[1536]{0:T(1024)S(1)}, f32[1536]{0:T(1024)S(1)}, f32[1536]{0:T(1024)S(1)}, f32[1536]{0:T(1024)S(1)}, /...) fusion(f32[2,12,12,1536]{3,2,1,0:T(8,128)S(1)} %convert_multipl, ...), kind=kLoop, calls=%fused_computation.63 | loop fusion | flops 19436544 | bytes 7200384 | tf_op jit(solution)/shard_map/reduce_sum | solution.py:85
  580.3 6.3 multiply_reduce_fusion.19
  586.6 5.4 multiply_reduce_fusion.38
  592.8 4.8 stack.207
  597.6 0.0 all-gather.10.cloned.1.call-update
  597.6 0.0 all-reduce.6.cloned.1.call-start
  597.7 36.3 %all-gather.10.cloned.1.call-done = f32[8,51,1536]{2,1,0:T(8,128)} async-done(((f32[1,51,1536]{2,1,0:T(8,128)}), f32[8,51,1536]{2,1,0:T(8,128)}) %all-gather.10.cloned.1.call-update) | async-done | bytes 2506768 | tf_op jit(solution)/shard_map/all_gather | solution.py:91
  633.9 2.0 reduce_sum.591
  635.9 0.7 multiply_reduce_fusion.54
  636.6 5.5 psum.62
  642.8 0.8 broadcast_multiply_fusion.1
  643.6 0.0 all-reduce.6.cloned.1.call-update
  643.6 5.5 fusion.2
  649.2 18.2 %all-reduce.6.cloned.1.call-done = f32[51,1536]{1,0:T(8,128)} async-done(((f32[51,1536]{1,0:T(8,128)}), f32[51,1536]{1,0:T(8,128)}) %all-reduce.6.cloned.1.call-update) | async-done | bytes 313360 | tf_op jit(solution)/shard_map/psum | solution.py:94
  667.4 1.0 broadcast_multiply_fusion
  668.4 0.6 slice_reduce_fusion
  669.0 0.8 reshape.170
  (74 shorter events, 0.4 us)
Async XLA Ops:
  7.2 201.4 %all-gather.6.cloned.1.call-start = ((), (), s32[]{:S(2)}) async-start(), calls=%async_computation.3 | async-start | bytes 24772608 | tf_op jit(solution)/shard_map/all_gather | solution.py:53
  11.6 0.7 copy-start.9
  11.6 1.0 copy-start.2
  11.6 2.6 copy-start
  11.7 306.2 %reduce-scatter.2.cloned.1.call-start = ((), (), s32[]{:S(2)}) async-start(), calls=%async_computation.4 | async-start | bytes 12386304 | tf_op jit(solution)/shard_map/reduce_scatter | solution.py:55
  47.9 0.6 copy-start.3
  47.9 0.6 copy-start.5
  325.5 5.0 copy-start.10
  325.5 58.1 %all-to-all-start = ((bf16[8,36,3584]{2,1,0:T(8,128)(2,1)}), bf16[8,36,3584]{2,1,0:T(8,128)(2,1)}, u32[]{:S(2)}, u32[]{:S(2)}) async-start(bf16[8,36,3584]{2,1,0:T(8,128)(2,1)} %all_to_all.14), calls=%async_computation.1 | async-start | bytes 4587520 | tf_op jit(solution)/shard_map/all_to_all | solution.py:58
  330.3 213.5 %all-gather.8.cloned.1.call-start = ((), (), s32[]{:S(2)}) async-start(), calls=%async_computation.5 | async-start | bytes 6193152 | tf_op jit(solution)/shard_map/all_gather | solution.py:71
  387.7 9.2 %copy-start.7 = (f32[3584]{0:T(1024)S(1)}, f32[3584]{0:T(1024)}, u32[]{:S(2)}) copy-start(f32[3584]{0:T(1024)} %param.18) | copy-start | bytes 43012
  485.6 58.1 %copy-start.8 = (f32[1536]{0:T(1024)S(1)}, f32[1536]{0:T(1024)}, u32[]{:S(2)}) copy-start(f32[1536]{0:T(1024)} %param.13) | copy-start | bytes 18436
  489.6 144.3 %all-gather.10.cloned.1.call-start = ((), (), s32[]{:S(2)}) async-start(), calls=%async_computation.7 | async-start | bytes 3096576 | tf_op jit(solution)/shard_map/all_gather | solution.py:91
  557.0 2.8 copy-start.4
  557.0 2.8 copy-start.6
  580.3 6.4 copy-start.1
  597.6 69.8 %all-reduce.6.cloned.1.call-start = ((), (), s32[]{:S(2)}) async-start(), calls=%async_computation.6 | async-start | bytes 688128 | tf_op jit(solution)/shard_map/psum | solution.py:94
Sparse Core Ops, SparseCore 0:
  11.8 196.7 all-gather.5
  221.8 96.0 reduce-scatter.1
  489.8 53.9 all-gather.7
  597.7 36.1 all-gather.9
  643.7 23.5 all-reduce.5
